TPU v7x, 256 devices: a whole 4x4x8 slice. The times are simulated.
256 devices in a mesh: expert: 32 (over x, z), tensor: 8 (over y, core).
Axes of the slice: x: 4, y: 4, z: 8, core: 2. Of those that a mesh axis runs over, the one named last changes fastest.
Arguments:
- tokens: bfloat16 [4096, 4096], P('expert', 'tensor'), may hold values from -3 to 3
- norm_gain: float32 [4096], replicated, may hold values from 0.1 to 1.9
- w_gate: bfloat16 [64, 1536, 4096], P('expert', 'tensor'), may hold values from -0.09375 to 0.09375
- w_up: bfloat16 [64, 1536, 4096], P('expert', 'tensor'), may hold values from -0.09375 to 0.09375
- w_down: bfloat16 [64, 1536, 4096], P('expert', 'tensor'), may hold values from -0.15625 to 0.15625
- routes: int32 [4096, 8], P('expert'), may hold values from 0 to 63, all different within a row; in each aligned block of 128 rows (0 to 127, 128 to 255, ...) at most 24 rows name the same one
- shares: int32 [4096, 8], P('expert'), may hold values from 1 to 32
- skipped: int32 [4096], P('expert'), may hold values 0 or 1
Outputs:
- mixed: bfloat16 [4096, 4096], P('expert', 'tensor')
Inputs may be any that keep to these rules, and one draw needn't show every extreme that they name: In each aligned block of 128 rows (the rows of one index of expert), no expert is named by more than 24 of the block's routes, and in every draw some block names some expert exactly 24 times; a row names 8 different experts.
All inputs are finite; a program needn't handle non-finite values. No bound on the sum of `skipped` on one device may be relied on, other than what follows from the above.
Results may differ from a plain program's by a relative error of at most 0.012.
Values may be sent and summed in bfloat16 or wider, within the bound.
A program may use at most 128 MiB of HBM per device.

v0:
```python
import jax
import jax.numpy as jnp
from jax import lax
from jax.sharding import PartitionSpec as P


def body(tokens, norm_gain, w_gate, w_up, w_down, routes, shares, skipped):
    groups = lax.axis_size("expert")
    tparts = lax.axis_size("tensor")
    tok_rows = routes.shape[0]
    top_k = routes.shape[1]
    local_exp = w_gate.shape[0]
    all_exp = local_exp * groups
    capacity = tok_rows * top_k * 3 // (2 * all_exp)
    slice_feat = tokens.shape[1]
    full_feat = slice_feat * tparts
    flat = routes.reshape(-1)
    onehot = (flat[:, None] == jnp.arange(all_exp, dtype=jnp.int32)[None, :]).astype(jnp.int32)
    rank = jnp.sum(jnp.cumsum(onehot, axis=0) * onehot, axis=1) - 1
    position = flat * capacity + rank
    owner = jnp.arange(tok_rows * top_k, dtype=jnp.int32) // top_k
    weights = shares.astype(jnp.float32)
    coef = weights / jnp.sum(weights, axis=1, keepdims=True)
    coef = coef * (1.0 - skipped.astype(jnp.float32))[:, None]
    values = tokens.astype(jnp.float32)
    whole = lax.all_gather(tokens, "tensor", axis=1, tiled=True).astype(jnp.float32)
    meansq = jnp.mean(whole * whole, axis=1, keepdims=True)
    normed = (whole * lax.rsqrt(meansq + 1e-06) * norm_gain).astype(jnp.bfloat16)
    outgoing = (
        jnp.zeros((all_exp * capacity, full_feat), jnp.bfloat16).at[position].set(normed[owner])
    )
    outgoing = outgoing.reshape(groups, local_exp * capacity, full_feat)
    arrived = lax.all_to_all(outgoing, "expert", split_axis=0, concat_axis=0, tiled=True)
    arrived = arrived.reshape(groups, local_exp, capacity, full_feat)
    gate = jnp.einsum("secd,efd->secf", arrived, w_gate, preferred_element_type=jnp.float32)
    upper = jnp.einsum("secd,efd->secf", arrived, w_up, preferred_element_type=jnp.float32)
    hidden = (jax.nn.silu(gate) * upper).astype(jnp.bfloat16)
    partial_out = jnp.einsum("secf,efd->secd", hidden, w_down, preferred_element_type=jnp.float32)
    rounded = partial_out.astype(jnp.bfloat16)
    back = lax.all_to_all(
        rounded.reshape(groups, local_exp * capacity, full_feat),
        "expert",
        split_axis=0,
        concat_axis=0,
        tiled=True,
    )
    picked = back.reshape(all_exp * capacity, full_feat)[position].astype(jnp.float32)
    mixed_full = jnp.einsum("tkd,tk->td", picked.reshape(tok_rows, top_k, full_feat), coef)
    moe = lax.psum_scatter(
        mixed_full.astype(jnp.bfloat16), "tensor", scatter_dimension=1, tiled=True
    ).astype(jnp.float32)
    return (values + moe).astype(jnp.bfloat16)


def solution(mesh):
    return jax.shard_map(
        body,
        mesh=mesh,
        in_specs=(
            P("expert", "tensor"),
            P(),
            P("expert", "tensor", None),
            P("expert", "tensor", None),
            P("expert", "tensor", None),
            P("expert", None),
            P("expert", None),
            P("expert"),
        ),
        out_specs=P("expert", "tensor"),
        check_vma=False,
    )
```

profile of v0, /device:TPU:8, one launch (start us, length us, event | category | flops | bytes accessed | tf_op | source)
XLA Modules:
  0.0 789.2 jit_solution(9588099414131480300)
XLA Ops:
  6.5 0.7 all-gather.2.cloned.1.call-update
  7.3 1.0 copy.10
  8.5 0.7 fusion.29
  9.2 30.8 %reduce-window.6 = s32[64,8,128]{2,1,0:T(8,128)S(1)} reduce-window(s32[64,8,128]{2,1,0:T(8,128)} %fusion.29, s32[]{:T(128)} %constant.34.clone.1), window={size=1x1x128 pad=0_0x0_0x127_0}, to_apply=%region_0.0 | reduce-window | flops 8323072 | bytes 524292 | tf_op jit(solution)/shard_map/reduce-window
  40.0 0.9 slice.12
  40.9 1.1 copy.12
  42.1 0.7 broadcast_multiply_fusion
  43.0 0.1 broadcast_add_fusion
  43.3 1.5 fusion.11
  44.8 2.6 fusion.13
  47.4 16.4 %gather_fusion = bf16[1024,4096]{1,0:T(8,128)(2,1)} fusion(bf16[128,4096]{1,0:T(8,128)(2,1)} %fusion.13, s32[1024]{0:T(1024)S(1)} %broadcast_clamp_fusion.1), kind=kCustom, calls=%fused_computation | custom fusion | bytes 16781312 | tf_op jit(solution)/shard_map/gather | solution.py:30
  63.8 19.8 %scatter_custom_fusion = bf16[1536,4096]{1,0:T(8,128)(2,1)} fusion(s32[1024]{0:T(1024)S(1)} %bitcast.79, bf16[1024,4096]{1,0:T(8,128)(2,1)} %gather_fusion, bf16[]{:T(256)} %constant.32.clone.1), kind=kCustom, calls=%fused_computation.10 | custom fusion | bytes 12583424 | tf_op jit(solution)/shard_map/scatter | solution.py:30
  83.6 287.2 %all_to_all.10 = bf16[32,48,4096]{2,1,0:T(8,128)(2,1)} all-to-all(bf16[32,48,4096]{2,1,0:T(8,128)(2,1)} %bitcast.73), channel_id=1, replica_groups=mesh['expert'=32,'tensor'=8] {'expert'}, dimensions={0} | all-to-all | bytes 25165824 | tf_op jit(solution)/shard_map/all_to_all | solution.py:33
  370.9 10.1 %fusion.2 = f32[2,32,24,192]{3,2,1,0:T(8,128)} fusion(bf16[32,2,24,4096]{3,2,1,0:T(8,128)(2,1)} %bitcast.74, bf16[2,192,4096]{2,1,0:T(8,128)(2,1)} %param.10), kind=kOutput, calls=%fused_computation.6 | convolution fusion | flops 2415919104 | bytes 16908288 | tf_op jit(solution)/shard_map/secd,efd->secf/dot_general | solution.py:35
  381.0 19.4 %convert_bitcast_fusion = bf16[32,2,24,4096]{3,2,0,1:T(8,128)(2,1)} fusion(bf16[2,192,4096]{2,1,0:T(8,128)(2,1)S(1)} %copy-done, f32[2,32,24,192]{3,2,1,0:T(8,128)} %fusion.2, bf16[2,192,4096]{2,1,0:T(8,128)(2,1)} %param.11, bf16[32,2,24,4096]{3,2,1,0:T(8,128)(2,1)} %bitcast.75), kind=kOutput, calls=%fused_computation.3 | convolution fusion | flops 4839899136 | bytes 32636928 | tf_op jit(solution)/shard_map/secf,efd->secd/dot_general | solution.py:38
  400.4 10.7 %copy.15 = bf16[32,2,24,4096]{3,2,1,0:T(8,128)(2,1)} copy(bf16[32,2,24,4096]{3,2,0,1:T(8,128)(2,1)} %convert_bitcast_fusion) | data formatting | bytes 25165824 | tf_op jit(solution)/shard_map/convert_element_type | solution.py:39
  411.1 5.3 all-to-all-start.1
  416.4 0.3 reduce-scatter.2.cloned.1.call-start
  416.9 283.0 %all-to-all-done.1 = bf16[32,48,4096]{2,1,0:T(8,128)(2,1)} async-done(((bf16[32,48,4096]{2,1,0:T(8,128)(2,1)}), bf16[32,48,4096]{2,1,0:T(8,128)(2,1)}, u32[]{:S(2)}, u32[]{:S(2)}) %all-to-all-start.1) | async-done | bytes 12582944 | tf_op jit(solution)/shard_map/all_to_all | solution.py:40
  699.9 21.4 %gather_fusion.1 = bf16[1024,4096]{1,0:T(8,128)(2,1)} fusion(bf16[1536,4096]{1,0:T(8,128)(2,1)} %bitcast.17, s32[1024]{0:T(1024)S(1)} %broadcast_clamp_fusion), kind=kCustom, calls=%fused_computation.1 | custom fusion | bytes 16781312 | tf_op jit(solution)/shard_map/gather | solution.py:47
  721.3 7.1 fusion.4
  728.4 3.7 copy.32
  732.1 48.6 %reduce-scatter.2.cloned.1.call-done = bf16[128,512]{1,0:T(8,128)(2,1)} async-done(((bf16[128,4096]{1,0:T(8,128)(2,1)}), bf16[128,512]{1,0:T(8,128)(2,1)}) %reduce-scatter.2.cloned.1.call-update) | async-done | bytes 131088 | tf_op jit(solution)/shard_map/reduce_scatter | solution.py:49
  780.8 1.6 add_convert_fusion
  (31 shorter events, 0.8 us)
Async XLA Ops:
  6.5 374.5 %copy-start = (bf16[2,192,4096]{2,1,0:T(8,128)(2,1)S(1)}, bf16[2,192,4096]{2,1,0:T(8,128)(2,1)}, u32[]{:S(2)}) copy-start(bf16[2,192,4096]{2,1,0:T(8,128)(2,1)} %param.12) | copy-start | bytes 9437188
  6.5 36.7 %all-gather.2.cloned.1.call-start = ((), (), s32[]{:S(2)}) async-start(), calls=%async_computation.3 | async-start | bytes 1179648 | tf_op jit(solution)/shard_map/all_gather | solution.py:26
  411.1 5.6 copy-start.3
  411.1 5.6 copy-start.4
  411.1 288.8 %all-to-all-start.1 = ((bf16[32,48,4096]{2,1,0:T(8,128)(2,1)}), bf16[32,48,4096]{2,1,0:T(8,128)(2,1)}, u32[]{:S(2)}, u32[]{:S(2)}) async-start(bf16[32,48,4096]{2,1,0:T(8,128)(2,1)} %bitcast.72), calls=%async_computation.1 | async-start | bytes 25165824 | tf_op jit(solution)/shard_map/all_to_all | solution.py:40
  416.4 364.3 %reduce-scatter.2.cloned.1.call-start = ((), (), s32[]{:S(2)}) async-start(), calls=%async_computation.4 | async-start | bytes 1179648 | tf_op jit(solution)/shard_map/reduce_scatter | solution.py:49
  699.9 82.5 %copy-start.1 = (bf16[2,192,4096]{2,1,0:T(8,128)(2,1)S(1)}, bf16[2,192,4096]{2,1,0:T(8,128)(2,1)}, u32[]{:S(2)}) copy-start(bf16[2,192,4096]{2,1,0:T(8,128)(2,1)} %param.12) | copy-start | bytes 9437188
  721.3 59.5 %copy-start.2 = (bf16[128,512]{1,0:T(8,128)(2,1)S(1)}, bf16[128,512]{1,0:T(8,128)(2,1)}, u32[]{:S(2)}) copy-start(bf16[128,512]{1,0:T(8,128)(2,1)} %param.8) | copy-start | bytes 393220
Sparse Core Ops, SparseCore 0:
  9.2 27.2 all-gather.1
  732.3 48.4 reduce-scatter.1
where the time goes:
time: 794 us; the launch traced here: 789 us
  waiting for transfers between devices  332 us (42%)
  blocking collectives  287 us (36%)
  local copies, waits for them, and re-layouts  75.6 us (10%)
  other arithmetic  38.3 us (5%)
  matrix products  36.6 us (5%)
  between operations  13.5 us (2%)
    all_to_all x1, blocking collectives, body(): lax.all_to_all(outgoing, 'expert', split_axis=0, concat_axis=0, tiled=True)  287 us
    all_to_all x1, waiting for transfers between devices, body(): lax.all_to_all(rounded.reshape(groups, local_exp * capacity, full_feat),...  283 us
    reduce_scatter x1, waiting for transfers between devices, body(): lax.psum_scatter(mixed_full.astype(jnp.bfloat16), 'tensor', scatter_dimen...  48.6 us
    another operation x3, other arithmetic  31 us
    gather x1, local copies, waits for them, and re-layouts, body(): back.reshape(all_exp * capacity, full_feat)[position].astype(jnp.float32)  21.4 us
    scatter x1, local copies, waits for them, and re-layouts, body(): jnp.zeros((all_exp * capacity, full_feat), jnp.bfloat16).at[position]  19.8 us
    dot_general x1, matrix products, body(): jnp.einsum('secf,efd->secd', hidden, w_down, preferred_element_type=jnp.f...  19.4 us
    gather x1, local copies, waits for them, and re-layouts, body(): normed[owner]  16.4 us
  transfers between devices with their start and end apart: 3, of which 2 were waited for; matrix products, arithmetic and copies ran while one was open for 5% of the time, Pallas kernels for 0%

commit v1 on v0

v1 whole, which is shorter than its diff:
```python
import jax
import jax.numpy as jnp
from jax import lax
from jax.sharding import PartitionSpec as P


def slot_tables(routes, coef, inv_rms, all_exp, capacity):
    tok_rows = routes.shape[0]
    hit = routes[:, :, None] == jnp.arange(all_exp, dtype=jnp.int32)[None, None, :]
    named = jnp.any(hit, axis=1)
    weight = jnp.sum(jnp.where(hit, coef[:, :, None], 0.0), axis=1)
    before = jnp.cumsum(named.astype(jnp.int32), axis=0) - 1
    slot = jnp.arange(capacity, dtype=jnp.int32)
    put = named.T[:, None, :] & (before.T[:, None, :] == slot[None, :, None])
    ids = jnp.arange(tok_rows, dtype=jnp.float32)
    token = jnp.sum(jnp.where(put, ids[None, None, :], 0.0), axis=2)
    scale = jnp.sum(jnp.where(put, weight.T[:, None, :], 0.0), axis=2)
    norm = jnp.sum(jnp.where(put, inv_rms[None, None, :], 0.0), axis=2)
    return jnp.stack([token, scale, norm], axis=0)


def body(tokens, norm_gain, w_gate, w_up, w_down, routes, shares, skipped):
    groups = lax.axis_size("expert")
    tparts = lax.axis_size("tensor")
    tok_rows, top_k = routes.shape
    local_exp = w_gate.shape[0]
    all_exp = local_exp * groups
    capacity = tok_rows * top_k * 3 // (2 * all_exp)
    slice_feat = tokens.shape[1]
    full_feat = slice_feat * tparts
    me = lax.axis_index("tensor")

    weights = shares.astype(jnp.float32)
    coef = weights / jnp.sum(weights, axis=1, keepdims=True)
    coef = coef * (1.0 - skipped.astype(jnp.float32))[:, None]

    values = tokens.astype(jnp.float32)
    gain = lax.dynamic_slice(norm_gain, (me * slice_feat,), (slice_feat,))
    scaled = (values * gain[None, :]).astype(jnp.bfloat16)
    sumsq = lax.psum(jnp.sum(values * values, axis=1), "tensor")
    inv_rms = lax.rsqrt(sumsq / full_feat + 1e-06)

    tables = slot_tables(routes, coef, inv_rms, all_exp, capacity)
    tables = tables.reshape(3, groups, local_exp * capacity).transpose(1, 0, 2).reshape(groups, -1)
    tables = lax.all_to_all(tables, "expert", split_axis=0, concat_axis=0, tiled=True)
    tables = tables.reshape(groups, 3, local_exp, capacity)
    rows = groups * capacity
    block = jnp.arange(groups, dtype=jnp.int32)[:, None, None] * tok_rows
    token = (tables[:, 0].astype(jnp.int32) + block).transpose(1, 0, 2).reshape(-1)
    scale = tables[:, 1].transpose(1, 0, 2).reshape(-1)
    norm = tables[:, 2].transpose(1, 0, 2).reshape(local_exp, rows)

    every = lax.all_gather(scaled, "expert", axis=0, tiled=True)
    picked = every[token]
    full = lax.all_gather(picked, "tensor", axis=1, tiled=True).reshape(local_exp, rows, full_feat)
    gate = jnp.einsum("erd,efd->erf", full, w_gate, preferred_element_type=jnp.float32) * norm[:, :, None]
    upper = jnp.einsum("erd,efd->erf", full, w_up, preferred_element_type=jnp.float32) * norm[:, :, None]
    hidden = (jax.nn.silu(gate) * upper).astype(jnp.bfloat16)
    partial_out = jnp.einsum("erf,efd->erd", hidden, w_down, preferred_element_type=jnp.float32)
    rounded = partial_out.astype(jnp.bfloat16).reshape(local_exp * rows, full_feat)
    summed = lax.psum_scatter(rounded, "tensor", scatter_dimension=1, tiled=True)
    weighted = summed.astype(jnp.float32) * scale[:, None]
    spread = jnp.zeros((groups * tok_rows, slice_feat), jnp.float32).at[token].add(weighted)
    moe = lax.psum_scatter(spread.astype(jnp.bfloat16), "expert", scatter_dimension=0, tiled=True)
    return (values + moe.astype(jnp.float32)).astype(jnp.bfloat16)


def solution(mesh):
    return jax.shard_map(
        body,
        mesh=mesh,
        in_specs=(
            P("expert", "tensor"),
            P(),
            P("expert", "tensor", None),
            P("expert", "tensor", None),
            P("expert", "tensor", None),
            P("expert", None),
            P("expert", None),
            P("expert"),
        ),
        out_specs=P("expert", "tensor"),
        check_vma=False,
    )
```

time: 794 us -> 522 us (0.66)
  blocking collectives: 287 us -> 11.8 us
  waiting for transfers between devices: 332 us -> 419 us
  local copies, waits for them, and re-layouts: 75.6 us -> 10.7 us
  other arithmetic: 38.3 us -> 28.4 us
  matrix products: 36.6 us -> 26.8 us
    all_to_all x1 -> x0, blocking collectives: 287 us -> none  [body(): lax.all_to_all(outgoing, 'expert', split_axis=0, concat_axis=0, tiled=True)]
    all_to_all x1, waiting for transfers between devices: 283 us -> 9.87 us  [body(): lax.all_to_all(tables, 'expert', split_axis=0, concat_axis=0, tiled=True)]
    reduce_scatter x1 -> x2, waiting for transfers between devices: 48.6 us -> 296 us  [the longest x1 223 us: body(): lax.psum_scatter(spread.astype(jnp.bfloat16), 'expert', scatter_dimension...]
    all_gather x1 -> x2, waiting for transfers between devices: 0.02 us -> 113 us  [the longest x1 66.7 us: body(): lax.all_gather(picked, 'tensor', axis=1, tiled=True)]
    another operation x3 -> x1, other arithmetic: 31 us -> 0.17 us  [slot_tables(): before = jnp.cumsum(named.astype(jnp.int32), axis=0) - 1]
    gather x2 -> x1, local copies, waits for them, and re-layouts: 37.8 us -> 8.2 us  [body(): picked = every[token]]
    scatter x1 -> x0, local copies, waits for them, and re-layouts: 19.8 us -> none  [body(): jnp.zeros((all_exp * capacity, full_feat), jnp.bfloat16).at[position]]
    scatter-add x0 -> x1, other arithmetic: none -> 14.6 us  [body(): jnp.zeros((groups * tok_rows, slice_feat), jnp.float32).at[token]]
  transfers between devices with their start and end apart: 3 -> 5, of which waited for: 2 -> 5; matrix products, arithmetic and copies ran while one was open for 5% -> 1% of each run, Pallas kernels for 0% -> 0%
where the time goes in v1:
time: 522 us
  waiting for transfers between devices  419 us (80%)
  other arithmetic  28.4 us (5%)
  matrix products  26.8 us (5%)
  between operations  13.3 us (3%)
  blocking collectives  11.8 us (2%)
  starting transfers between devices  11.6 us (2%)
  local copies, waits for them, and re-layouts  10.7 us (2%)
    reduce_scatter x1, waiting for transfers between devices, body(): lax.psum_scatter(spread.astype(jnp.bfloat16), 'expert', scatter_dimension...  223 us
    reduce_scatter x1, waiting for transfers between devices, body(): lax.psum_scatter(rounded, 'tensor', scatter_dimension=1, tiled=True)  73.3 us
    all_gather x1, waiting for transfers between devices, body(): lax.all_gather(picked, 'tensor', axis=1, tiled=True)  66.7 us
    all_gather x1, waiting for transfers between devices, body(): every = lax.all_gather(scaled, 'expert', axis=0, tiled=True)  46.3 us
    dot_general x1, matrix products, body(): jnp.einsum('erf,efd->erd', hidden, w_down, preferred_element_type=jnp.flo...  16 us
    scatter-add x1, other arithmetic, body(): jnp.zeros((groups * tok_rows, slice_feat), jnp.float32).at[token]  14.6 us
    psum x1, blocking collectives, body(): sumsq = lax.psum(jnp.sum(values * values, axis=1), 'tensor')  11.8 us
    all_to_all x1, starting transfers between devices, body(): lax.all_to_all(tables, 'expert', split_axis=0, concat_axis=0, tiled=True)  11.3 us
  transfers between devices with their start and end apart: 5, of which 5 were waited for; matrix products, arithmetic and copies ran while one was open for 1% of the time, Pallas kernels for 0%

profile of v1, /device:TPU:8, one launch (start us, length us, event | category | flops | bytes accessed | tf_op | source)
XLA Modules:
  0.0 522.0 jit_solution(12121312157993786148)
XLA Ops:
  6.5 0.9 dynamic_slice.3
  7.4 1.6 fusion.16
  9.1 0.7 fusion.18
  10.0 0.2 reduce_window_sum.11
  10.2 11.8 %psum.7 = f32[128]{0:T(128)S(1)} all-reduce(f32[128]{0:T(128)S(1)} %get-tuple-element.9), channel_id=1, replica_groups=mesh['expert'=32,'tensor'=8] {'tensor'}, use_global_device_ids=true, to_apply=%region_7.8 | all-reduce | flops 128 | bytes 1024 | tf_op jit(solution)/shard_map/psum | solution.py:40
  22.1 0.7 convert_reduce_fusion
  22.8 0.7 convert_subtract_fusion
  23.4 0.7 divide_multiply_fusion
  24.1 0.7 select_reduce_fusion.3
  24.8 0.7 select_reduce_fusion.2
  25.9 0.7 all_to_all.8
  26.6 11.3 %all-to-all-start = ((f32[32,1,144]{2,1,0:T(1,128)}), f32[32,1,144]{2,1,0:T(1,128)S(1)}, u32[]{:S(2)}, u32[]{:S(2)}) async-start(f32[32,1,144]{2,1,0:T(1,128)} %all_to_all.8), calls=%async_computation | async-start | bytes 65536 | tf_op jit(solution)/shard_map/all_to_all | solution.py:45
  38.0 9.9 %all-to-all-done = f32[32,1,144]{2,1,0:T(1,128)S(1)} async-done(((f32[32,1,144]{2,1,0:T(1,128)}), f32[32,1,144]{2,1,0:T(1,128)S(1)}, u32[]{:S(2)}, u32[]{:S(2)}) %all-to-all-start) | async-done | bytes 18464 | tf_op jit(solution)/shard_map/all_to_all | solution.py:45
  48.3 46.3 %all-gather.4.cloned.1.call-done = bf16[4096,512]{1,0:T(8,128)(2,1)} async-done(((bf16[128,512]{1,0:T(8,128)(2,1)}), bf16[4096,512]{1,0:T(8,128)(2,1)}) %all-gather.4.cloned.1.call-update) | async-done | bytes 4194320 | tf_op jit(solution)/shard_map/all_gather | solution.py:53
  94.6 8.2 %gather_fusion = bf16[1536,512]{1,0:T(8,128)(2,1)} fusion(bf16[4096,512]{1,0:T(8,128)(2,1)} %all-gather.4.cloned.1.call-done, s32[2048]{0:T(1024)S(1)} %pad_clamp_fusion), kind=kCustom, calls=%fused_computation | custom fusion | bytes 3151872 | tf_op jit(solution)/shard_map/gather | solution.py:54
  103.0 66.7 %all-gather.6.cloned.1.call-done = bf16[1536,4096]{1,0:T(8,128)(2,1)} async-done(((bf16[1536,512]{1,0:T(8,128)(2,1)}), bf16[1536,4096]{1,0:T(8,128)(2,1)}) %all-gather.6.cloned.1.call-update) | async-done | bytes 12582928 | tf_op jit(solution)/shard_map/all_gather | solution.py:55
  169.7 10.8 %convolution_multiply_fusion.1 = f32[2,768,192]{1,2,0:T(8,128)} fusion(bf16[2,768,4096]{2,1,0:T(8,128)(2,1)} %bitcast.32, bf16[2,192,4096]{2,1,0:T(8,128)(2,1)} %param.10, f32[2,768]{1,0:T(2,128)S(1)} %mul.74), kind=kOutput, calls=%fused_computation.9 | convolution fusion | flops 2416214016 | bytes 16914432 | tf_op jit(solution)/shard_map/erd,efd->erf/dot_general | solution.py:56
  180.5 16.0 %convolution_convert_fusion = bf16[2,768,4096]{2,1,0:T(8,128)(2,1)} fusion(bf16[2,192,4096]{2,1,0:T(8,128)(2,1)S(1)} %copy-done, bf16[2,768,4096]{2,1,0:T(8,128)(2,1)} %bitcast.33, bf16[2,192,4096]{2,1,0:T(8,128)(2,1)} %param.11, f32[2,768,192]{1,2,0:T(8,128)} %convolution_multiply_fusion.1, f32[2,768]{1,0:T(2,128)S(1)} %mul.74), kind=kOutput, calls=%fused_computation.2 | convolution fusion | flops 4840194048 | bytes 32643072 | tf_op jit(solution)/shard_map/erf,efd->erd/dot_general | solution.py:59
  196.5 0.2 reduce-scatter.5.cloned.1.call-start
  196.8 73.3 %reduce-scatter.3.cloned.1.call-done = bf16[1536,512]{1,0:T(8,128)(2,1)} async-done(((bf16[1536,4096]{1,0:T(8,128)(2,1)}), bf16[1536,512]{1,0:T(8,128)(2,1)}) %reduce-scatter.3.cloned.1.call-update) | async-done | bytes 1572880 | tf_op jit(solution)/shard_map/reduce_scatter | solution.py:61
  270.2 14.6 %scatter_custom_fusion = f32[4096,512]{1,0:T(8,128)} fusion(s32[1536]{0:T(1024)S(1)} %fusion.22, f32[]{:T(128)} %constant.11.clone.1, bf16[1536,512]{1,0:T(8,128)(2,1)} %reduce-scatter.3.cloned.1.call-done, f32[1536]{0:T(1024)S(1)} %mul.80), kind=kCustom, calls=%fused_computation.3 | custom fusion | flops 2359296 | bytes 9969668 | tf_op jit(solution)/shard_map/scatter-add | solution.py:63
  284.8 5.9 %convert_element_type.49 = bf16[4096,512]{1,0:T(8,128)(2,1)} convert(f32[4096,512]{1,0:T(8,128)} %scatter_custom_fusion) | non-fusion elementwise | flops 2097152 | bytes 12582912 | tf_op jit(solution)/shard_map/convert_element_type | solution.py:64
  290.7 223.1 %reduce-scatter.5.cloned.1.call-done = bf16[128,512]{1,0:T(8,128)(2,1)} async-done(((bf16[4096,512]{1,0:T(8,128)(2,1)}), bf16[128,512]{1,0:T(8,128)(2,1)}) %reduce-scatter.5.cloned.1.call-update) | async-done | bytes 131088 | tf_op jit(solution)/shard_map/reduce_scatter | solution.py:64
  513.8 1.6 fusion.17
  (34 shorter events, 1.2 us)
Async XLA Ops:
  6.5 174.0 %copy-start = (bf16[2,192,4096]{2,1,0:T(8,128)(2,1)S(1)}, bf16[2,192,4096]{2,1,0:T(8,128)(2,1)}, u32[]{:S(2)}) copy-start(bf16[2,192,4096]{2,1,0:T(8,128)(2,1)} %param.12) | copy-start | bytes 9437188
  6.5 88.1 %all-gather.4.cloned.1.call-start = ((), (), s32[]{:S(2)}) async-start(), calls=%async_computation.3 | async-start | bytes 4325376 | tf_op jit(solution)/shard_map/all_gather | solution.py:53
  26.6 21.3 %all-to-all-start = ((f32[32,1,144]{2,1,0:T(1,128)}), f32[32,1,144]{2,1,0:T(1,128)S(1)}, u32[]{:S(2)}, u32[]{:S(2)}) async-start(f32[32,1,144]{2,1,0:T(1,128)} %all_to_all.8), calls=%async_computation | async-start | bytes 65536 | tf_op jit(solution)/shard_map/all_to_all | solution.py:45
  37.9 131.8 %all-gather.6.cloned.1.call-start = ((), (), s32[]{:S(2)}) async-start(), calls=%async_computation.6 | async-start | bytes 14155776 | tf_op jit(solution)/shard_map/all_gather | solution.py:55
  102.8 167.4 %reduce-scatter.3.cloned.1.call-start = ((), (), s32[]{:S(2)}) async-start(), calls=%async_computation.4 | async-start | bytes 14155776 | tf_op jit(solution)/shard_map/reduce_scatter | solution.py:61
  196.5 317.3 %reduce-scatter.5.cloned.1.call-start = ((), (), s32[]{:S(2)}) async-start(), calls=%async_computation.5 | async-start | bytes 4325376 | tf_op jit(solution)/shard_map/reduce_scatter | solution.py:64
  290.7 223.1 %copy-start.1 = (bf16[128,512]{1,0:T(8,128)(2,1)S(1)}, bf16[128,512]{1,0:T(8,128)(2,1)}, u32[]{:S(2)}) copy-start(bf16[128,512]{1,0:T(8,128)(2,1)} %param.8) | copy-start | bytes 393220
Sparse Core Ops, SparseCore 0:
  10.0 84.6 all-gather.3
  103.0 66.6 all-gather.5
  196.6 73.5 reduce-scatter.2
  290.9 222.9 reduce-scatter.4

commit v2 on v0

v2 whole, which is shorter than its diff:
```python
import functools

import jax
import jax.numpy as jnp
from jax import lax
from jax.experimental import pallas as pl
from jax.experimental.pallas import tpu as pltpu
from jax.sharding import PartitionSpec as P

MESH = pl.DeviceIdType.MESH
LINE_Z = 8
CORES = 2
F32 = jnp.float32
BF16 = jnp.bfloat16


def kernel(
    nx, nz, ny, cap, full_feat,
    tokens_ref, gain_ref, routes_ref, shares_ref, skipped_ref, wg_hbm, wu_hbm, wd_hbm,
    out_ref,
    wg, wu, wd, sums, pick, share, normed, outgoing, rows_in, acc, part, pair_in, line_in, done, back, total,
    w_sem, sum_send, sum_recv, disp_send, disp_recv, ag_send, ag_recv,
    pair_send, pair_recv, line_send, line_recv, ret_send, ret_recv,
):
    ne = nx * nz
    nt = ny * CORES
    tok = tokens_ref.shape[0]
    feat = tokens_ref.shape[1]
    two = wg.shape[0]
    blk = 2 * cap
    chunk = nx * blk
    e = lax.axis_index("expert")
    t = lax.axis_index("tensor")
    x, z = e // nz, e % nz
    y, c = t // CORES, t % CORES
    sib = y * CORES + (1 - c)

    def shift(p):
        j, dx = p // nx, p % nx
        half, odd = (j + 1) // 2, j % 2
        return dx, odd * half + (1 - odd) * ((nz - half) % nz)

    def expert_peer(p, sign):
        dx, dz = shift(p)
        return ((x + sign * dx + nx) % nx) * nz + (z + sign * dz + nz) % nz

    def tensor_peer(dy, core):
        return ((y + dy + ny) % ny) * CORES + core

    barrier = pltpu.get_barrier_semaphore()

    def greet_e(p, _):
        pl.semaphore_signal(barrier, inc=1, device_id=(expert_peer(p, 1), t), device_id_type=MESH)
        return 0

    def greet_t(k, _):
        pl.semaphore_signal(barrier, inc=1, device_id=(e, (t + k) % nt), device_id_type=MESH)
        return 0

    weights = [
        pltpu.make_async_copy(hbm, vmem, w_sem.at[i])
        for i, (hbm, vmem) in enumerate(((wg_hbm, wg), (wu_hbm, wu), (wd_hbm, wd)))
    ]
    for copy in weights:
        copy.start()
    lax.fori_loop(1, ne, greet_e, 0)
    lax.fori_loop(1, nt, greet_t, 0)

    eye = (
        lax.broadcasted_iota(jnp.int32, (tok, tok), 0) == lax.broadcasted_iota(jnp.int32, (tok, tok), 1)
    ).astype(F32)
    values = tokens_ref[...].astype(F32)
    column = jnp.sum(values * values, axis=1, keepdims=True)
    row = jnp.sum(eye * column, axis=0, keepdims=True)
    sums[0] = jnp.broadcast_to(row, (8, tok))
    pl.semaphore_wait(barrier, ne - 1 + nt - 1)

    def sum_copy(k):
        return pltpu.make_async_remote_copy(
            sums.at[0], sums.at[k], sum_send.at[k], sum_recv.at[k],
            device_id=(e, (t + k) % nt), device_id_type=MESH,
        )

    def start_sum(k, _):
        sum_copy(k).start()
        return 0

    lax.fori_loop(1, nt, start_sum, 0)

    def turned(ref):
        return lax.dot_general(
            ref[...].astype(F32).astype(BF16), eye.astype(BF16), (((0,), (0,)), ((), ())),
            preferred_element_type=F32,
        )

    routes_t, shares_t = turned(routes_ref), turned(shares_ref)
    ids = lax.broadcasted_iota(jnp.int32, (2 * ne, tok), 0)
    expert_id = (2 * expert_peer(ids // 2, 1) + ids % 2).astype(F32)
    named = jnp.zeros((2 * ne, tok), F32)
    weight = jnp.zeros((2 * ne, tok), F32)
    for k in range(routes_t.shape[0]):
        hit = (expert_id == routes_t[k : k + 1, :]).astype(F32)
        named = named + hit
        weight = weight + hit * shares_t[k : k + 1, :]
    earlier = (
        lax.broadcasted_iota(jnp.int32, (tok, tok), 0) < lax.broadcasted_iota(jnp.int32, (tok, tok), 1)
    ).astype(F32).astype(BF16)
    slot = lax.dot_general(
        named.astype(BF16), earlier, (((1,), (0,)), ((), ())), preferred_element_type=F32
    )
    slot = jnp.where(named > 0.0, slot, -1.0)
    place = lax.broadcasted_iota(jnp.int32, (cap, tok), 0).astype(F32)
    for r in range(2 * ne):
        match = (slot[r : r + 1, :] == place).astype(F32)
        pick[r * cap : (r + 1) * cap, :] = match
        share[r * cap : (r + 1) * cap, :] = match * weight[r : r + 1, :]

    def wait_sum(k, square):
        sum_copy(k).wait()
        return square + sums[k, 0:1, :]

    square = lax.fori_loop(1, nt, wait_sum, row)
    factor = lax.rsqrt(square * (1.0 / full_feat) + 1e-06)
    factor = jnp.sum(eye * factor, axis=1, keepdims=True)
    gain = gain_ref[pl.ds(t, 1), :]
    normed[...] = (values * factor * gain).astype(BF16)

    def dispatch(p):
        rows = pl.ds(p * blk, blk)
        return pltpu.make_async_remote_copy(
            outgoing.at[rows], rows_in.at[t, rows], disp_send.at[p], disp_recv.at[p],
            device_id=(expert_peer(p, 1), t), device_id_type=MESH,
        )

    def select(j, _):
        rows = pl.ds(j * chunk, chunk)
        outgoing[rows, :] = jnp.dot(
            pick[rows, :].astype(BF16), normed[...], preferred_element_type=F32
        ).astype(BF16)

        def start(i, _):
            p = j * nx + i

            @pl.when(p > 0)
            def _():
                dispatch(p).start()

            return 0

        return lax.fori_loop(0, nx, start, 0)

    lax.fori_loop(0, nz, select, 0)
    rows_in[t, 0:blk, :] = outgoing[0:blk, :]

    def gather(j, k):
        rows = pl.ds(j * chunk, chunk)
        if k == 0:
            source, target = t, sib
        elif k < ny:
            source, target = t, tensor_peer(k, c)
        else:
            source, target = tensor_peer(-(k - ny + 1), c), sib
        return pltpu.make_async_remote_copy(
            rows_in.at[source, rows], rows_in.at[source, rows], ag_send.at[j, k], ag_recv.at[j, k],
            device_id=(e, target), device_id_type=MESH,
        )

    def gathered(j, k):
        rows = pl.ds(j * chunk, chunk)
        if k == 0:
            source = sib
        elif k < ny:
            source = tensor_peer(-k, c)
        else:
            source = tensor_peer(-(k - ny + 1), 1 - c)
        return pltpu.make_async_remote_copy(
            rows_in.at[source, rows], rows_in.at[source, rows], ag_send.at[j, k], ag_recv.at[j, k],
            device_id=(e, sib), device_id_type=MESH,
        )

    def pair(j):
        rows = pl.ds(j * chunk, chunk)
        return pltpu.make_async_remote_copy(
            part.at[1 - c, :, rows], pair_in.at[:, rows], pair_send.at[j], pair_recv.at[j],
            device_id=(e, sib), device_id_type=MESH,
        )

    def line(j, dy):
        rows = pl.ds(j * chunk, chunk)
        return pltpu.make_async_remote_copy(
            part.at[c, (y + dy) % ny, rows], line_in.at[dy - 1, rows],
            line_send.at[j, dy - 1], line_recv.at[j, dy - 1],
            device_id=(e, tensor_peer(dy, c)), device_id_type=MESH,
        )

    def give_back(p):
        rows = pl.ds(p * blk, blk)
        return pltpu.make_async_remote_copy(
            done.at[rows], back.at[rows], ret_send.at[p], ret_recv.at[p],
            device_id=(expert_peer(p, -1), t), device_id_type=MESH,
        )

    def stage_gather(j):
        def arrived(i, _):
            p = j * nx + i

            @pl.when(p > 0)
            def _():
                dispatch(p).wait_recv()

            return 0

        lax.fori_loop(0, nx, arrived, 0)
        for k in range(ny):
            gather(j, (k + 1) % ny).start()

    def stage_forward(j):
        for k in range(1, ny):
            gathered(j, k).wait_recv()
            gather(j, ny - 1 + k).start()

    def stage_expert(j):
        @pl.when(j == 0)
        def _():
            for copy in weights:
                copy.wait()

        gathered(j, 0).wait_recv()
        for k in range(ny, 2 * ny - 1):
            gathered(j, k).wait_recv()
        rows = pl.ds(j * chunk, chunk)
        acc[...] = jnp.zeros_like(acc)

        def up(s, _):
            cols = pl.ds(pl.multiple_of(s * feat, feat), feat)
            block = rows_in[s, rows, :]
            nt_dims = (((1,), (1,)), ((), ()))
            acc[0] += lax.dot_general(block, wg[:, cols], nt_dims, preferred_element_type=F32)
            acc[1] += lax.dot_general(block, wu[:, cols], nt_dims, preferred_element_type=F32)
            return 0

        lax.fori_loop(0, nt, up, 0)
        first_row = lax.broadcasted_iota(jnp.int32, (chunk, two), 0) % blk < cap
        first_col = lax.broadcasted_iota(jnp.int32, (chunk, two), 1) < two // 2
        gate = acc[0]
        hidden = gate * jax.nn.sigmoid(gate) * acc[1]
        hidden = jnp.where(first_row == first_col, hidden, 0.0).astype(BF16)

        def down(s, _):
            cols = pl.ds(pl.multiple_of(s * feat, feat), feat)
            part[s % CORES, s // CORES, rows, :] = jnp.dot(
                hidden, wd[:, cols], preferred_element_type=F32
            ).astype(BF16)
            return 0

        lax.fori_loop(0, nt, down, 0)
        pair(j).start()

    def stage_pair(j):
        rows = pl.ds(j * chunk, chunk)
        pair(j).wait_recv()
        for dy in range(1, ny):
            to = (y + dy) % ny
            part[c, to, rows, :] = (
                part[c, to, rows, :].astype(F32) + pair_in[to, rows, :].astype(F32)
            ).astype(BF16)
            line(j, dy).start()

    def stage_line(j):
        rows = pl.ds(j * chunk, chunk)
        result = part[c, y, rows, :].astype(F32) + pair_in[y, rows, :].astype(F32)
        for dy in range(1, ny):
            line(j, dy).wait_recv()
            result = result + line_in[dy - 1, rows, :].astype(F32)
        done[rows, :] = result.astype(BF16)

        def start(i, _):
            p = j * nx + i

            @pl.when(p > 0)
            def _():
                give_back(p).start()

            return 0

        lax.fori_loop(0, nx, start, 0)

        @pl.when(j == 0)
        def _():
            back[0:blk, :] = done[0:blk, :]

    def stage_mix(j):
        rows = pl.ds(j * chunk, chunk)

        def arrived(i, _):
            p = j * nx + i

            @pl.when(p > 0)
            def _():
                give_back(p).wait_recv()

            return 0

        lax.fori_loop(0, nx, arrived, 0)
        total[...] += lax.dot_general(
            share[rows, :].astype(BF16), back[rows, :], (((0,), (0,)), ((), ())),
            preferred_element_type=F32,
        )

    total[...] = jnp.zeros_like(total)
    stages = (
        (0, stage_gather), (1, stage_forward), (2, stage_expert), (3, stage_pair), (5, stage_line), (7, stage_mix),
    )

    def step(i, _):
        for lag, stage in stages:
            @pl.when((i >= lag) & (i < nz + lag))
            def _(lag=lag, stage=stage):
                stage(i - lag)

        return 0

    lax.fori_loop(0, nz + stages[-1][0], step, 0)

    lax.fori_loop(1, ne, lambda p, _: (dispatch(p).wait_send(), give_back(p).wait_send(), 0)[2], 0)

    def drain(j, _):
        for k in range(2 * ny - 1):
            gather(j, k).wait_send()
        pair(j).wait_send()
        for dy in range(1, ny):
            line(j, dy).wait_send()
        return 0

    lax.fori_loop(0, nz, drain, 0)

    of_shares = jnp.sum(shares_ref[...].astype(F32), axis=1, keepdims=True)
    skip = jnp.sum(eye * skipped_ref[...].astype(F32), axis=1, keepdims=True)
    out_ref[...] = (values + total[...] / of_shares * (1.0 - skip)).astype(BF16)


def body(tokens, norm_gain, w_gate, w_up, w_down, routes, shares, skipped):
    ne = lax.axis_size("expert")
    nt = lax.axis_size("tensor")
    nz = LINE_Z
    nx = ne // nz
    ny = nt // CORES
    tok, feat = tokens.shape
    top = routes.shape[1]
    local, ff, full = w_gate.shape
    cap = tok * top * 3 // (2 * local * ne)
    rows = ne * local * cap
    chunk = nx * local * cap
    flat = [w.reshape(local * ff, full) for w in (w_gate, w_up, w_down)]
    vmem = pl.BlockSpec(memory_space=pltpu.VMEM)
    hbm = pl.BlockSpec(memory_space=pl.ANY)
    dma = pltpu.SemaphoreType.DMA
    return pl.pallas_call(
        functools.partial(kernel, nx, nz, ny, cap, full),
        out_shape=jax.ShapeDtypeStruct((tok, feat), BF16),
        in_specs=[vmem] * 5 + [hbm] * 3,
        out_specs=vmem,
        scratch_shapes=[
            pltpu.VMEM((local * ff, full), BF16),
            pltpu.VMEM((local * ff, full), BF16),
            pltpu.VMEM((local * ff, full), BF16),
            pltpu.VMEM((nt, 8, tok), F32),
            pltpu.VMEM((rows, tok), F32),
            pltpu.VMEM((rows, tok), F32),
            pltpu.VMEM((tok, feat), BF16),
            pltpu.VMEM((rows, feat), BF16),
            pltpu.VMEM((nt, rows, feat), BF16),
            pltpu.VMEM((2, chunk, local * ff), F32),
            pltpu.VMEM((CORES, ny, rows, feat), BF16),
            pltpu.VMEM((ny, rows, feat), BF16),
            pltpu.VMEM((ny - 1, rows, feat), BF16),
            pltpu.VMEM((rows, feat), BF16),
            pltpu.VMEM((rows, feat), BF16),
            pltpu.VMEM((tok, feat), F32),
            dma((3,)),
            dma((nt,)),
            dma((nt,)),
            dma((ne,)),
            dma((ne,)),
            dma((nz, 2 * ny - 1)),
            dma((nz, 2 * ny - 1)),
            dma((nz,)),
            dma((nz,)),
            dma((nz, ny - 1)),
            dma((nz, ny - 1)),
            dma((ne,)),
            dma((ne,)),
        ],
        compiler_params=pltpu.CompilerParams(
            collective_id=0, has_side_effects=True, vmem_limit_bytes=60 * 2**20
        ),
    )(tokens, norm_gain.reshape(nt, feat), routes, shares, skipped.reshape(1, tok), *flat)


def solution(mesh):
    return jax.shard_map(
        body,
        mesh=mesh,
        in_specs=(
            P("expert", "tensor"),
            P(),
            P("expert", "tensor", None),
            P("expert", "tensor", None),
            P("expert", "tensor", None),
            P("expert", None),
            P("expert", None),
            P("expert"),
        ),
        out_specs=P("expert", "tensor"),
        check_vma=False,
    )
```

time: 794 us -> 188 us (0.24)
  waiting for transfers between devices: 332 us -> 0 us
  blocking collectives: 287 us -> 0 us
  Pallas kernels: 0 us -> 181 us
  local copies, waits for them, and re-layouts: 75.6 us -> 5.71 us
  other arithmetic: 38.3 us -> 0 us
  matrix products: 36.6 us -> 0 us
  between operations: 13.5 us -> 0.01 us
    all_to_all x1 -> x0, blocking collectives: 287 us -> none  [body(): lax.all_to_all(outgoing, 'expert', split_axis=0, concat_axis=0, tiled=True)]
    all_to_all x1 -> x0, waiting for transfers between devices: 283 us -> none  [body(): lax.all_to_all(rounded.reshape(groups, local_exp * capacity, full_feat),...]
    pallas_call x0 -> x1, Pallas kernels: none -> 181 us  [body(): pl.pallas_call(functools.partial(kernel, nx, nz, ny, cap, full), out_shap...]
    reduce_scatter x1 -> x0, waiting for transfers between devices: 48.6 us -> none  [body(): lax.psum_scatter(mixed_full.astype(jnp.bfloat16), 'tensor', scatter_dimen...]
    gather x2 -> x0, local copies, waits for them, and re-layouts: 37.8 us -> none  [the longest x1 21.4 us: body(): back.reshape(all_exp * capacity, full_feat)[position].astype(jnp.float32)]
    dot_general x3 -> x0, matrix products: 36.6 us -> none  [the longest x1 19.4 us: body(): jnp.einsum('secf,efd->secd', hidden, w_down, preferred_element_type=jnp.f...]
    another operation x3 -> x0, other arithmetic: 31 us -> none
    scatter x1 -> x0, local copies, waits for them, and re-layouts: 19.8 us -> none  [body(): jnp.zeros((all_exp * capacity, full_feat), jnp.bfloat16).at[position]]
  transfers between devices with their start and end apart: 3 -> 0, of which waited for: 2 -> 0; matrix products, arithmetic and copies ran while one was open for 5% -> 0% of each run, Pallas kernels for 0% -> 0%
where the time goes in v2:
time: 188 us; the launch traced here: 186 us
  Pallas kernels  181 us (96%)
  local copies, waits for them, and re-layouts  5.71 us (3%)
    pallas_call x1, Pallas kernels, body(): pl.pallas_call(functools.partial(kernel, nx, nz, ny, cap, full), out_shap...  181 us
    unnamed x3, local copies, waits for them, and re-layouts  4.39 us

profile of v2, /device:TPU:8, one launch (start us, length us, event | category | flops | bytes accessed | tf_op | source)
XLA Modules:
  0.0 186.3 jit_solution(14529684385464178955)
XLA Ops:
  0.0 1.3 reshape.15.gain_ref
  1.3 1.4 copy.9.routes_ref
  2.7 1.4 copy.10.shares_ref
  4.1 180.6 %shard_map.82 = bf16[128,512]{1,0:T(8,128)(2,1)} custom-call(bf16[128,512]{1,0:T(8,128)(2,1)} %tokens_ref.1, f32[8,512]{1,0:T(8,128)} %reshape.15.gain_ref, s32[128,8]{1,0:T(8,128)} %copy.9.routes_ref, s32[128,8]{1,0:T(8,128)} %copy.10.shares_ref, s32[1,128]{1,0:T(1,128)} %bitcast.7, bf16[384,4096]{1,0:T(8,128)(2,1)} %bitcast.4, bf16[384,4096]{1,0:T(8,128)(2,1)} %bitcast.5, ...), custom_call_target="tpu_custom_call" | custom-call | tf_op jit(solution)/shard_map/pallas_call | solution.py:358
  184.7 1.6 copy.12

commit v3 on v2

v3 whole, which is shorter than its diff:
```python
import functools

import jax
import jax.numpy as jnp
from jax import lax
from jax.experimental import pallas as pl
from jax.experimental.pallas import tpu as pltpu
from jax.sharding import PartitionSpec as P

MESH = pl.DeviceIdType.MESH
LINE_Z = 8
CORES = 2
F32 = jnp.float32
BF16 = jnp.bfloat16


def kernel(
    nx, nz, ny, cap, full_feat,
    tokens_ref, gain_ref, routes_ref, shares_ref, skipped_ref, wg_hbm, wu_hbm, wd_hbm,
    out_ref,
    wg, wu, wd, sums, pick, share, normed, outgoing, rows_in, acc, part, pair_in, hop_in, line_in, done, back, total,
    w_sem, sum_send, sum_recv, disp_send, disp_recv, ag_send, ag_recv, fw_send, fw_recv,
    pair_send, pair_recv, hop_send, hop_recv, line_send, line_recv, ret_send, ret_recv,
):
    ne = nx * nz
    nt = ny * CORES
    tok = tokens_ref.shape[0]
    feat = tokens_ref.shape[1]
    two = wg.shape[0]
    blk = 2 * cap
    chunk = nx * blk
    e = lax.axis_index("expert")
    t = lax.axis_index("tensor")
    x, z = e // nz, e % nz
    y, c = t // CORES, t % CORES
    sib = y * CORES + (1 - c)

    order = [1, nz - 1, 2, nz - 2, 4, 3, nz - 3, 0] if nz == 8 else list(range(1, nz)) + [0]
    local = order.index(0)

    def wrap(v, n):
        v = jnp.where(v >= n, v - n, v)
        return jnp.where(v < 0, v + n, v)

    def offset(j):
        if isinstance(j, int):
            return order[j]
        return sum(jnp.where(j == k, dz, 0) for k, dz in enumerate(order))

    def expert_peer(j, dx, sign):
        return wrap(x + sign * dx, nx) * nz + wrap(z + sign * offset(j), nz)

    def tensor_peer(dy, core):
        return wrap(y + dy, ny) * CORES + core

    barrier = pltpu.get_barrier_semaphore()

    weights = [
        pltpu.make_async_copy(hbm, vmem, w_sem.at[i])
        for i, (hbm, vmem) in enumerate(((wg_hbm, wg), (wu_hbm, wu), (wd_hbm, wd)))
    ]
    for copy in weights:
        copy.start()
    for k in range(1, nt):
        pl.semaphore_signal(barrier, inc=1, device_id=(e, wrap(t + k, nt)), device_id_type=MESH)
    for j in range(nz):
        for dx in range(nx):
            if j != local or dx:
                pl.semaphore_signal(barrier, inc=1, device_id=(expert_peer(j, dx, 1), t), device_id_type=MESH)

    eye = (
        lax.broadcasted_iota(jnp.int32, (tok, tok), 0) == lax.broadcasted_iota(jnp.int32, (tok, tok), 1)
    ).astype(F32)
    values = tokens_ref[...].astype(F32)
    column = jnp.sum(values * values, axis=1, keepdims=True)
    row = jnp.sum(eye * column, axis=0, keepdims=True)
    sums[0] = jnp.broadcast_to(row, (8, tok))
    pl.semaphore_wait(barrier, ne - 1 + nt - 1)

    def sum_copy(k):
        return pltpu.make_async_remote_copy(
            sums.at[0], sums.at[k], sum_send.at[k], sum_recv.at[k],
            device_id=(e, wrap(t + k, nt)), device_id_type=MESH,
        )

    for k in range(1, nt):
        sum_copy(k).start()

    routes_t, shares_t = routes_ref[...].astype(F32), shares_ref[...].astype(F32)
    ids = lax.broadcasted_iota(jnp.int32, (2 * ne, tok), 0)
    expert_id = (2 * expert_peer(ids // (2 * nx), ids // 2 % nx, 1) + ids % 2).astype(F32)
    named = jnp.zeros((2 * ne, tok), F32)
    weight = jnp.zeros((2 * ne, tok), F32)
    for k in range(routes_t.shape[0]):
        hit = (expert_id == routes_t[k : k + 1, :]).astype(F32)
        named = named + hit
        weight = weight + hit * shares_t[k : k + 1, :]
    earlier = (
        lax.broadcasted_iota(jnp.int32, (tok, tok), 0) < lax.broadcasted_iota(jnp.int32, (tok, tok), 1)
    ).astype(F32).astype(BF16)
    slot = lax.dot_general(
        named.astype(BF16), earlier, (((1,), (0,)), ((), ())), preferred_element_type=F32
    )
    slot = jnp.where(named > 0.0, slot, -1.0)
    place = lax.broadcasted_iota(jnp.int32, (cap, tok), 0).astype(F32)
    for r in range(2 * ne):
        match = (slot[r : r + 1, :] == place).astype(F32)
        pick[r * cap : (r + 1) * cap, :] = match
        share[r * cap : (r + 1) * cap, :] = match * weight[r : r + 1, :]

    square = row
    for k in range(1, nt):
        sum_copy(k).wait()
        square = square + sums[k, 0:1, :]
    factor = lax.rsqrt(square * (1.0 / full_feat) + 1e-06)
    factor = jnp.sum(eye * factor, axis=1, keepdims=True)
    lanes = gain_ref.shape[1]
    for q in range(feat // lanes):
        cols = slice(q * lanes, (q + 1) * lanes)
        gain = gain_ref[pl.ds(t * (feat // lanes) + q, 1), :]
        normed[:, cols] = (values[:, cols] * factor * gain).astype(BF16)

    def block(j, dx):
        return pl.ds(j * chunk + dx * blk, blk)

    def dispatch(j, dx):
        return pltpu.make_async_remote_copy(
            outgoing.at[block(j, dx)], rows_in.at[t, block(j, dx)], disp_send.at[j, dx], disp_recv.at[j, dx],
            device_id=(expert_peer(j, dx, 1), t), device_id_type=MESH,
        )

    def give_back(j, dx):
        return pltpu.make_async_remote_copy(
            done.at[block(j, dx)], back.at[block(j, dx)], ret_send.at[j, dx], ret_recv.at[j, dx],
            device_id=(expert_peer(j, dx, -1), t), device_id_type=MESH,
        )

    def each(j, act):
        pl.when(j != local)(lambda: act(0))
        for dx in range(1, nx):
            act(dx)

    def stage_send(j):
        rows = whole(j)
        outgoing[rows, :] = jnp.dot(
            pick[rows, :].astype(BF16), normed[...], preferred_element_type=F32
        ).astype(BF16)
        each(j, lambda dx: dispatch(j, dx).start())

        @pl.when(j == local)
        def _():
            rows_in[t, block(j, 0), :] = outgoing[block(j, 0), :]

    up, down, far = tensor_peer(1, c), tensor_peer(-1, c), tensor_peer(2, c)
    half = chunk // 2

    def along(source, rows, send, recv, target):
        return pltpu.make_async_remote_copy(
            rows_in.at[source, rows], rows_in.at[source, rows], send, recv,
            device_id=(e, target), device_id_type=MESH,
        )

    def whole(j):
        return pl.ds(j * chunk, chunk)

    def piece(j, h):
        return pl.ds(j * chunk + h * half, half)

    def own_up(j, source):
        return along(source, whole(j), ag_send.at[j, 0], ag_recv.at[j, 0], up)

    def own_down(j, source):
        return along(source, whole(j), ag_send.at[j, 1], ag_recv.at[j, 1], down)

    def on_up(j, source):
        return along(source, piece(j, 0), ag_send.at[j, 2], ag_recv.at[j, 2], up)

    def on_down(j, source):
        return along(source, piece(j, 1), ag_send.at[j, 3], ag_recv.at[j, 3], down)

    def across(j, k, source):
        return along(source, whole(j), fw_send.at[j, k], fw_recv.at[j, k], sib)

    def pair(j):
        rows = pl.ds(j * chunk, chunk)
        return pltpu.make_async_remote_copy(
            part.at[1 - c, :, rows], pair_in.at[:, rows], pair_send.at[j], pair_recv.at[j],
            device_id=(e, sib), device_id_type=MESH,
        )

    def hop(j, h):
        return pltpu.make_async_remote_copy(
            part.at[c, (y + 2) % ny, piece(j, h)], hop_in.at[h, pl.ds(j * half, half)],
            hop_send.at[j, h], hop_recv.at[j, h],
            device_id=(e, down if h else up), device_id_type=MESH,
        )

    def line(j, h):
        return pltpu.make_async_remote_copy(
            part.at[c, (y + (ny - 1 if h else 1)) % ny, whole(j)], line_in.at[h, whole(j)],
            line_send.at[j, h], line_recv.at[j, h],
            device_id=(e, down if h else up), device_id_type=MESH,
        )

    def stage_gather(j):
        each(j, lambda dx: dispatch(j, dx).wait_recv())
        own_up(j, t).start()
        own_down(j, t).start()
        across(j, 0, t).start()

    def stage_forward(j):
        own_up(j, down).wait_recv()
        on_up(j, down).start()
        across(j, 1, down).start()
        own_down(j, up).wait_recv()
        on_down(j, up).start()
        across(j, 2, up).start()

    def stage_far(j):
        on_up(j, far).wait_recv()
        on_down(j, far).wait_recv()
        across(j, 3, far).start()

    def stage_expert(j):
        @pl.when(j == 0)
        def _():
            for copy in weights:
                copy.wait()

        for k, dy in enumerate((0, -1, 1, 2)):
            across(j, k, tensor_peer(dy, 1 - c)).wait_recv()
        rows = whole(j)
        acc[...] = jnp.zeros_like(acc)

        def widen(s, _):
            cols = pl.ds(pl.multiple_of(s * feat, feat), feat)
            lhs = rows_in[s, rows, :]
            nt_dims = (((1,), (1,)), ((), ()))
            acc[0] += lax.dot_general(lhs, wg[:, cols], nt_dims, preferred_element_type=F32)
            acc[1] += lax.dot_general(lhs, wu[:, cols], nt_dims, preferred_element_type=F32)
            return 0

        lax.fori_loop(0, nt, widen, 0)
        first_row = lax.broadcasted_iota(jnp.int32, (chunk, two), 0) % blk < cap
        first_col = lax.broadcasted_iota(jnp.int32, (chunk, two), 1) < two // 2
        gate = acc[0]
        hidden = gate * jax.nn.sigmoid(gate) * acc[1]
        hidden = jnp.where(first_row == first_col, hidden, 0.0).astype(BF16)

        def narrow(s, _):
            cols = pl.ds(pl.multiple_of(s * feat, feat), feat)
            part[s % CORES, s // CORES, rows, :] = jnp.dot(
                hidden, wd[:, cols], preferred_element_type=F32
            ).astype(BF16)
            return 0

        lax.fori_loop(0, nt, narrow, 0)
        pair(j).start()

    def stage_pair(j):
        rows = whole(j)
        pair(j).wait_recv()
        for dy in (2, 1, ny - 1):
            to = (y + dy) % ny
            part[c, to, rows, :] = (
                part[c, to, rows, :].astype(F32) + pair_in[to, rows, :].astype(F32)
            ).astype(BF16)
            if dy == 2:
                hop(j, 0).start()
                hop(j, 1).start()

    def stage_hop(j):
        for h in (0, 1):
            hop(j, h).wait_recv()
            to = (y + (ny - 1 if h else 1)) % ny
            rows = piece(j, h)
            part[c, to, rows, :] = (
                part[c, to, rows, :].astype(F32) + hop_in[h, pl.ds(j * half, half), :].astype(F32)
            ).astype(BF16)
            line(j, h).start()

    def stage_line(j):
        rows = whole(j)
        result = part[c, y, rows, :].astype(F32) + pair_in[y, rows, :].astype(F32)
        for h in (0, 1):
            line(j, h).wait_recv()
            result = result + line_in[h, rows, :].astype(F32)
        done[rows, :] = result.astype(BF16)

        each(j, lambda dx: give_back(j, dx).start())

        @pl.when(j == local)
        def _():
            back[block(j, 0), :] = done[block(j, 0), :]

    def stage_mix(j):
        rows = pl.ds(j * chunk, chunk)

        each(j, lambda dx: give_back(j, dx).wait_recv())
        total[...] += lax.dot_general(
            share[rows, :].astype(BF16), back[rows, :], (((0,), (0,)), ((), ())),
            preferred_element_type=F32,
        )

    total[...] = jnp.zeros_like(total)
    stages = (
        (0, stage_send), (2, stage_gather), (3, stage_forward), (4, stage_far), (5, stage_expert),
        (6, stage_pair), (7, stage_hop), (8, stage_line), (9, stage_mix),
    )

    def step(i, _):
        for lag, stage in stages:
            @pl.when((i >= lag) & (i < nz + lag))
            def _(lag=lag, stage=stage):
                stage(i - lag)

        return 0

    lax.fori_loop(0, nz + stages[-1][0], step, 0)

    def drain(j, _):
        each(j, lambda dx: (dispatch(j, dx).wait_send(), give_back(j, dx).wait_send())[0])
        own_up(j, t).wait_send()
        own_down(j, t).wait_send()
        on_up(j, down).wait_send()
        on_down(j, up).wait_send()
        for k, dy in enumerate((0, -1, 1, 2)):
            across(j, k, tensor_peer(dy, c)).wait_send()
        pair(j).wait_send()
        for h in (0, 1):
            hop(j, h).wait_send()
            line(j, h).wait_send()
        return 0

    lax.fori_loop(0, nz, drain, 0)

    keep = (1.0 - skipped_ref[...].astype(F32)) / jnp.sum(shares_ref[...].astype(F32), axis=0, keepdims=True)
    keep = jnp.sum(eye * keep, axis=1, keepdims=True)
    out_ref[...] = (tokens_ref[...].astype(F32) + total[...] * keep).astype(BF16)


def body(tokens, norm_gain, w_gate, w_up, w_down, routes, shares, skipped):
    ne = lax.axis_size("expert")
    nt = lax.axis_size("tensor")
    nz = LINE_Z
    nx = ne // nz
    ny = nt // CORES
    tok, feat = tokens.shape
    top = routes.shape[1]
    local, ff, full = w_gate.shape
    cap = tok * top * 3 // (2 * local * ne)
    rows = ne * local * cap
    chunk = nx * local * cap
    flat = [w.reshape(local * ff, full) for w in (w_gate, w_up, w_down)]
    vmem = pl.BlockSpec(memory_space=pltpu.VMEM)
    hbm = pl.BlockSpec(memory_space=pl.ANY)
    dma = pltpu.SemaphoreType.DMA
    return pl.pallas_call(
        functools.partial(kernel, nx, nz, ny, cap, full),
        out_shape=jax.ShapeDtypeStruct((tok, feat), BF16),
        in_specs=[vmem] * 5 + [hbm] * 3,
        out_specs=vmem,
        scratch_shapes=[
            pltpu.VMEM((local * ff, full), BF16),
            pltpu.VMEM((local * ff, full), BF16),
            pltpu.VMEM((local * ff, full), BF16),
            pltpu.VMEM((nt, 8, tok), F32),
            pltpu.VMEM((rows, tok), F32),
            pltpu.VMEM((rows, tok), F32),
            pltpu.VMEM((tok, feat), BF16),
            pltpu.VMEM((rows, feat), BF16),
            pltpu.VMEM((nt, rows, feat), BF16),
            pltpu.VMEM((2, chunk, local * ff), F32),
            pltpu.VMEM((CORES, ny, rows, feat), BF16),
            pltpu.VMEM((ny, rows, feat), BF16),
            pltpu.VMEM((2, rows // 2, feat), BF16),
            pltpu.VMEM((2, rows, feat), BF16),
            pltpu.VMEM((rows, feat), BF16),
            pltpu.VMEM((rows, feat), BF16),
            pltpu.VMEM((tok, feat), F32),
            dma((3,)),
            dma((nt,)),
            dma((nt,)),
            dma((nz, nx)),
            dma((nz, nx)),
            dma((nz, 4)),
            dma((nz, 4)),
            dma((nz, 4)),
            dma((nz, 4)),
            dma((nz,)),
            dma((nz,)),
            dma((nz, 2)),
            dma((nz, 2)),
            dma((nz, 2)),
            dma((nz, 2)),
            dma((nz, nx)),
            dma((nz, nx)),
        ],
        compiler_params=pltpu.CompilerParams(
            collective_id=0, has_side_effects=True, vmem_limit_bytes=60 * 2**20
        ),
    )(tokens, norm_gain.reshape(-1, 128), routes.T, shares.T, skipped.reshape(1, tok), *flat)


def solution(mesh):
    return jax.shard_map(
        body,
        mesh=mesh,
        in_specs=(
            P("expert", "tensor"),
            P(),
            P("expert", "tensor", None),
            P("expert", "tensor", None),
            P("expert", "tensor", None),
            P("expert", None),
            P("expert", None),
            P("expert"),
        ),
        out_specs=P("expert", "tensor"),
        check_vma=False,
    )
```

time: 188 us -> 148 us (0.79)
  Pallas kernels: 181 us -> 144 us
  local copies, waits for them, and re-layouts: 5.71 us -> 1.57 us
    pallas_call x1, Pallas kernels: 181 us -> 144 us  [body(): pl.pallas_call(functools.partial(kernel, nx, nz, ny, cap, full), out_shap...]
    unnamed x3 -> x1, local copies, waits for them, and re-layouts: 4.39 us -> 1.57 us
where the time goes in v3:
time: 148 us; the launch traced here: 145 us
  Pallas kernels  144 us (97%)
  local copies, waits for them, and re-layouts  1.57 us (1%)
    pallas_call x1, Pallas kernels, body(): pl.pallas_call(functools.partial(kernel, nx, nz, ny, cap, full), out_shap...  144 us

profile of v3, /device:TPU:8, one launch (start us, length us, event | category | flops | bytes accessed | tf_op | source)
XLA Modules:
  0.0 145.1 jit_solution(13919996957404510091)
XLA Ops:
  0.0 143.5 %shard_map.82 = bf16[128,512]{1,0:T(8,128)(2,1)} custom-call(bf16[128,512]{1,0:T(8,128)(2,1)} %tokens_ref.1, f32[32,128]{1,0:T(8,128)} %bitcast.10, s32[8,128]{1,0:T(8,128)} %bitcast.11, s32[8,128]{1,0:T(8,128)} %bitcast.12, s32[1,128]{1,0:T(1,128)} %bitcast.13, bf16[384,4096]{1,0:T(8,128)(2,1)} %bitcast.7, bf16[384,4096]{1,0:T(8,128)(2,1)} %bitcast.8, ...), custom_call_target="tpu_custom_call" | custom-call | tf_op jit(solution)/shard_map/pallas_call | solution.py:358
  143.6 1.6 %copy.10 = bf16[128,512]{1,0:T(8,128)(2,1)} copy(bf16[128,512]{1,0:T(8,128)(2,1)} %shard_map.82) | data formatting | bytes 262144

commit v4 on v3

--- a/solution.py
+++ b/solution.py
@@ -18,8 +18,8 @@
     nx, nz, ny, cap, full_feat,
     tokens_ref, gain_ref, routes_ref, shares_ref, skipped_ref, wg_hbm, wu_hbm, wd_hbm,
     out_ref,
-    wg, wu, wd, sums, pick, share, normed, outgoing, rows_in, acc, part, pair_in, hop_in, line_in, done, back, total,
-    w_sem, sum_send, sum_recv, disp_send, disp_recv, ag_send, ag_recv, fw_send, fw_recv,
+    wg, wu, wd, sums, slots, slot_share, pick, share, normed, outgoing, wide_out, rows_in, acc, part, pair_in, hop_in, line_in, done, back, wide_back, total, wide_total, red_out, red_in,
+    w_sem, sum_send, sum_recv, tok_send, tok_recv, red_send, red_recv, disp_send, disp_recv, ag_send, ag_recv, fw_send, fw_recv,
     pair_send, pair_recv, hop_send, hop_recv, line_send, line_recv, ret_send, ret_recv,
 ):
     ne = nx * nz
@@ -35,8 +35,11 @@
     y, c = t // CORES, t % CORES
     sib = y * CORES + (1 - c)
 
-    order = [1, nz - 1, 2, nz - 2, 4, 3, nz - 3, 0] if nz == 8 else list(range(1, nz)) + [0]
+    order = [nz - 1, 2, nz - 2, 4, 3, nz - 3, 1, 0] if nz == 8 else list(range(nz))
     local = order.index(0)
+
+    def is_wide(j):
+        return j == local
 
     def wrap(v, n):
         v = jnp.where(v >= n, v - n, v)
@@ -102,11 +105,8 @@
         named.astype(BF16), earlier, (((1,), (0,)), ((), ())), preferred_element_type=F32
     )
     slot = jnp.where(named > 0.0, slot, -1.0)
-    place = lax.broadcasted_iota(jnp.int32, (cap, tok), 0).astype(F32)
-    for r in range(2 * ne):
-        match = (slot[r : r + 1, :] == place).astype(F32)
-        pick[r * cap : (r + 1) * cap, :] = match
-        share[r * cap : (r + 1) * cap, :] = match * weight[r : r + 1, :]
+    slots[...] = slot
+    slot_share[...] = weight
 
     square = row
     for k in range(1, nt):
@@ -118,14 +118,40 @@
     for q in range(feat // lanes):
         cols = slice(q * lanes, (q + 1) * lanes)
         gain = gain_ref[pl.ds(t * (feat // lanes) + q, 1), :]
-        normed[:, cols] = (values[:, cols] * factor * gain).astype(BF16)
+        normed[y, :, cols] = (values[:, cols] * factor * gain).astype(BF16)
+
+    def token_copy(dy, row):
+        return pltpu.make_async_remote_copy(
+            normed.at[row], normed.at[row], tok_send.at[dy], tok_recv.at[dy],
+            device_id=(e, tensor_peer(dy, c)), device_id_type=MESH,
+        )
+
+    for dy in range(1, ny):
+        token_copy(dy, y).start()
 
     def block(j, dx):
         return pl.ds(j * chunk + dx * blk, blk)
 
+    def wide_block(dx):
+        return pl.ds(dx * blk, blk)
+
+    def wide_dispatch(j, dx):
+        return pltpu.make_async_remote_copy(
+            wide_out.at[:, wide_block(dx)], rows_in.at[c, :, block(j, dx)],
+            disp_send.at[j, dx], disp_recv.at[j, dx],
+            device_id=(expert_peer(j, dx, 1), t), device_id_type=MESH,
+        )
+
+    def wide_give_back(j, dx):
+        return pltpu.make_async_remote_copy(
+            part.at[c, :, block(j, dx)], wide_back.at[:, wide_block(dx)],
+            ret_send.at[j, dx], ret_recv.at[j, dx],
+            device_id=(expert_peer(j, dx, -1), t), device_id_type=MESH,
+        )
+
     def dispatch(j, dx):
         return pltpu.make_async_remote_copy(
-            outgoing.at[block(j, dx)], rows_in.at[t, block(j, dx)], disp_send.at[j, dx], disp_recv.at[j, dx],
+            outgoing.at[block(j, dx)], rows_in.at[c, y, block(j, dx)], disp_send.at[j, dx], disp_recv.at[j, dx],
             device_id=(expert_peer(j, dx, 1), t), device_id_type=MESH,
         )
 
@@ -142,22 +168,48 @@
 
     def stage_send(j):
         rows = whole(j)
-        outgoing[rows, :] = jnp.dot(
-            pick[rows, :].astype(BF16), normed[...], preferred_element_type=F32
-        ).astype(BF16)
-        each(j, lambda dx: dispatch(j, dx).start())
+        place = lax.broadcasted_iota(jnp.int32, (cap, tok), 0).astype(F32)
+        for r in range(2 * nx):
+            at = pl.ds(j * 2 * nx + r, 1)
+            match = (slots[at, :] == place).astype(F32)
+            pick[r * cap : (r + 1) * cap, :] = match
+            share[pl.ds(j * chunk + r * cap, cap), :] = match * slot_share[at, :]
+        chosen = pick[...].astype(BF16)
+
+        @pl.when(jnp.logical_not(is_wide(j)))
+        def _():
+            outgoing[rows, :] = jnp.dot(chosen, normed[y], preferred_element_type=F32).astype(BF16)
+            for dx in range(nx):
+                dispatch(j, dx).start()
 
         @pl.when(j == local)
         def _():
-            rows_in[t, block(j, 0), :] = outgoing[block(j, 0), :]
-
-    up, down, far = tensor_peer(1, c), tensor_peer(-1, c), tensor_peer(2, c)
+            for dy in range(1, ny):
+                token_copy(dy, wrap(y - dy, ny)).wait_recv()
+
+        @pl.when(is_wide(j))
+        def _():
+            def slices(k, _):
+                wide_out[k] = jnp.dot(
+                    chosen, normed[k], preferred_element_type=F32
+                ).astype(BF16)
+                return 0
+
+            lax.fori_loop(0, ny, slices, 0)
+            each(j, lambda dx: wide_dispatch(j, dx).start())
+
+        @pl.when(j == local)
+        def _():
+            for k in range(ny):
+                rows_in[c, k, block(j, 0), :] = wide_out[k, wide_block(0), :]
+
+    up, down = tensor_peer(1, c), tensor_peer(-1, c)
     half = chunk // 2
 
-    def along(source, rows, send, recv, target):
-        return pltpu.make_async_remote_copy(
-            rows_in.at[source, rows], rows_in.at[source, rows], send, recv,
-            device_id=(e, target), device_id_type=MESH,
+    def along(core, dy, rows, send, recv, target):
+        ref = rows_in.at[core, wrap(y + dy, ny), rows]
+        return pltpu.make_async_remote_copy(
+            ref, ref, send, recv, device_id=(e, target), device_id_type=MESH,
         )
 
     def whole(j):
@@ -166,20 +218,28 @@
     def piece(j, h):
         return pl.ds(j * chunk + h * half, half)
 
-    def own_up(j, source):
-        return along(source, whole(j), ag_send.at[j, 0], ag_recv.at[j, 0], up)
-
-    def own_down(j, source):
-        return along(source, whole(j), ag_send.at[j, 1], ag_recv.at[j, 1], down)
-
-    def on_up(j, source):
-        return along(source, piece(j, 0), ag_send.at[j, 2], ag_recv.at[j, 2], up)
-
-    def on_down(j, source):
-        return along(source, piece(j, 1), ag_send.at[j, 3], ag_recv.at[j, 3], down)
-
-    def across(j, k, source):
-        return along(source, whole(j), fw_send.at[j, k], fw_recv.at[j, k], sib)
+    def own_up(j, dy):
+        return along(c, dy, whole(j), ag_send.at[j, 0], ag_recv.at[j, 0], up)
+
+    def own_down(j, dy):
+        return along(c, dy, whole(j), ag_send.at[j, 1], ag_recv.at[j, 1], down)
+
+    def on_up(j, dy):
+        return along(c, dy, piece(j, 0), ag_send.at[j, 2], ag_recv.at[j, 2], up)
+
+    def on_down(j, dy):
+        return along(c, dy, piece(j, 1), ag_send.at[j, 3], ag_recv.at[j, 3], down)
+
+    def across(j, k, core, dy):
+        return along(core, dy, whole(j), fw_send.at[j, k], fw_recv.at[j, k], sib)
+
+    def wide_across(j, core):
+        ref = rows_in.at[core, :, whole(j)]
+        return pltpu.make_async_remote_copy(
+            ref, ref, fw_send.at[j, 0], fw_recv.at[j, 0], device_id=(e, sib), device_id_type=MESH,
+        )
+
+    turns = (0, -1, 1, 2)
 
     def pair(j):
         rows = pl.ds(j * chunk, chunk)
@@ -190,36 +250,48 @@
 
     def hop(j, h):
         return pltpu.make_async_remote_copy(
-            part.at[c, (y + 2) % ny, piece(j, h)], hop_in.at[h, pl.ds(j * half, half)],
+            part.at[c, wrap(y + 2, ny), piece(j, h)], hop_in.at[h, pl.ds(j * half, half)],
             hop_send.at[j, h], hop_recv.at[j, h],
             device_id=(e, down if h else up), device_id_type=MESH,
         )
 
     def line(j, h):
         return pltpu.make_async_remote_copy(
-            part.at[c, (y + (ny - 1 if h else 1)) % ny, whole(j)], line_in.at[h, whole(j)],
+            part.at[c, wrap(y + (-1 if h else 1), ny), whole(j)], line_in.at[h, whole(j)],
             line_send.at[j, h], line_recv.at[j, h],
             device_id=(e, down if h else up), device_id_type=MESH,
         )
 
     def stage_gather(j):
-        each(j, lambda dx: dispatch(j, dx).wait_recv())
-        own_up(j, t).start()
-        own_down(j, t).start()
-        across(j, 0, t).start()
+        @pl.when(is_wide(j))
+        def _():
+            each(j, lambda dx: wide_dispatch(j, dx).wait_recv())
+            wide_across(j, c).start()
+
+        @pl.when(jnp.logical_not(is_wide(j)))
+        def _():
+            for dx in range(nx):
+                dispatch(j, dx).wait_recv()
+            own_up(j, 0).start()
+            own_down(j, 0).start()
+            across(j, 0, c, 0).start()
 
     def stage_forward(j):
-        own_up(j, down).wait_recv()
-        on_up(j, down).start()
-        across(j, 1, down).start()
-        own_down(j, up).wait_recv()
-        on_down(j, up).start()
-        across(j, 2, up).start()
+        @pl.when(jnp.logical_not(is_wide(j)))
+        def _():
+            own_up(j, -1).wait_recv()
+            on_up(j, -1).start()
+            across(j, 1, c, -1).start()
+            own_down(j, 1).wait_recv()
+            on_down(j, 1).start()
+            across(j, 2, c, 1).start()
 
     def stage_far(j):
-        on_up(j, far).wait_recv()
-        on_down(j, far).wait_recv()
-        across(j, 3, far).start()
+        @pl.when(jnp.logical_not(is_wide(j)))
+        def _():
+            on_up(j, 2).wait_recv()
+            on_down(j, 2).wait_recv()
+            across(j, 3, c, 2).start()
 
     def stage_expert(j):
         @pl.when(j == 0)
@@ -227,14 +299,21 @@
             for copy in weights:
                 copy.wait()
 
-        for k, dy in enumerate((0, -1, 1, 2)):
-            across(j, k, tensor_peer(dy, 1 - c)).wait_recv()
+        @pl.when(is_wide(j))
+        def _():
+            wide_across(j, 1 - c).wait_recv()
+
+        @pl.when(jnp.logical_not(is_wide(j)))
+        def _():
+            for k, dy in enumerate(turns):
+                across(j, k, 1 - c, dy).wait_recv()
+
         rows = whole(j)
         acc[...] = jnp.zeros_like(acc)
 
         def widen(s, _):
             cols = pl.ds(pl.multiple_of(s * feat, feat), feat)
-            lhs = rows_in[s, rows, :]
+            lhs = rows_in[s % CORES, s // CORES, rows, :]
             nt_dims = (((1,), (1,)), ((), ()))
             acc[0] += lax.dot_general(lhs, wg[:, cols], nt_dims, preferred_element_type=F32)
             acc[1] += lax.dot_general(lhs, wu[:, cols], nt_dims, preferred_element_type=F32)
@@ -260,26 +339,48 @@
     def stage_pair(j):
         rows = whole(j)
         pair(j).wait_recv()
-        for dy in (2, 1, ny - 1):
-            to = (y + dy) % ny
+
+        def join(dy):
+            to = wrap(y + dy, ny)
             part[c, to, rows, :] = (
                 part[c, to, rows, :].astype(F32) + pair_in[to, rows, :].astype(F32)
             ).astype(BF16)
-            if dy == 2:
-                hop(j, 0).start()
-                hop(j, 1).start()
+
+        join(2)
+
+        @pl.when(jnp.logical_not(is_wide(j)))
+        def _():
+            hop(j, 0).start()
+            hop(j, 1).start()
+
+        join(1)
+        join(-1)
+
+        @pl.when(is_wide(j))
+        def _():
+            join(0)
+            each(j, lambda dx: wide_give_back(j, dx).start())
+
+        @pl.when(j == local)
+        def _():
+            wide_back[:, wide_block(0), :] = part[c, :, block(j, 0), :]
 
     def stage_hop(j):
-        for h in (0, 1):
-            hop(j, h).wait_recv()
-            to = (y + (ny - 1 if h else 1)) % ny
-            rows = piece(j, h)
-            part[c, to, rows, :] = (
-                part[c, to, rows, :].astype(F32) + hop_in[h, pl.ds(j * half, half), :].astype(F32)
-            ).astype(BF16)
-            line(j, h).start()
+        @pl.when(jnp.logical_not(is_wide(j)))
+        def _():
+            for h in (0, 1):
+                hop(j, h).wait_recv()
+                to = wrap(y + (-1 if h else 1), ny)
+                rows = piece(j, h)
+                part[c, to, rows, :] = (
+                    part[c, to, rows, :].astype(F32) + hop_in[h, pl.ds(j * half, half), :].astype(F32)
+                ).astype(BF16)
+                line(j, h).start()
 
     def stage_line(j):
+        pl.when(jnp.logical_not(is_wide(j)))(lambda: finish(j))
+
+    def finish(j):
         rows = whole(j)
         result = part[c, y, rows, :].astype(F32) + pair_in[y, rows, :].astype(F32)
         for h in (0, 1):
@@ -287,25 +388,72 @@
             result = result + line_in[h, rows, :].astype(F32)
         done[rows, :] = result.astype(BF16)
 
-        each(j, lambda dx: give_back(j, dx).start())
+        for dx in range(nx):
+            give_back(j, dx).start()
+
+    def reduce(dy):
+        return pltpu.make_async_remote_copy(
+            red_out.at[dy - 1], red_in.at[dy - 1], red_send.at[dy - 1], red_recv.at[dy - 1],
+            device_id=(e, tensor_peer(dy, c)), device_id_type=MESH,
+        )
+
+    def stage_mix(j):
+        rows = whole(j)
+        mine = share[rows, :].astype(BF16)
+        onto = (((0,), (0,)), ((), ()))
+
+        @pl.when(is_wide(j))
+        def _():
+            each(j, lambda dx: wide_give_back(j, dx).wait_recv())
+
+            def slices(k, _):
+                wide_total[k] += lax.dot_general(
+                    mine, wide_back[k], onto, preferred_element_type=F32
+                )
+                return 0
+
+            lax.fori_loop(0, ny, slices, 0)
 
         @pl.when(j == local)
         def _():
-            back[block(j, 0), :] = done[block(j, 0), :]
-
-    def stage_mix(j):
-        rows = pl.ds(j * chunk, chunk)
-
-        each(j, lambda dx: give_back(j, dx).wait_recv())
-        total[...] += lax.dot_general(
-            share[rows, :].astype(BF16), back[rows, :], (((0,), (0,)), ((), ())),
-            preferred_element_type=F32,
-        )
+            for dy in (2, 1, ny - 1):
+                red_out[dy - 1] = wide_total[wrap(y + dy, ny)].astype(BF16)
+                reduce(dy).start()
+
+        @pl.when(jnp.logical_not(is_wide(j)))
+        def _():
+            for dx in range(nx):
+                give_back(j, dx).wait_recv()
+            total[...] += lax.dot_general(mine, back[rows, :], onto, preferred_element_type=F32)
+
+    def stage_drain(j):
+        pair(j).wait_send()
+
+        @pl.when(is_wide(j))
+        def _():
+            each(j, lambda dx: (wide_dispatch(j, dx).wait_send(), wide_give_back(j, dx).wait_send())[0])
+            wide_across(j, c).wait_send()
+
+        @pl.when(jnp.logical_not(is_wide(j)))
+        def _():
+            for dx in range(nx):
+                dispatch(j, dx).wait_send()
+                give_back(j, dx).wait_send()
+            own_up(j, 0).wait_send()
+            own_down(j, 0).wait_send()
+            on_up(j, -1).wait_send()
+            on_down(j, 1).wait_send()
+            for k, dy in enumerate(turns):
+                across(j, k, c, dy).wait_send()
+            for h in (0, 1):
+                hop(j, h).wait_send()
+                line(j, h).wait_send()
 
     total[...] = jnp.zeros_like(total)
+    wide_total[...] = jnp.zeros_like(wide_total)
     stages = (
         (0, stage_send), (2, stage_gather), (3, stage_forward), (4, stage_far), (5, stage_expert),
-        (6, stage_pair), (7, stage_hop), (8, stage_line), (9, stage_mix),
+        (6, stage_pair), (7, stage_hop), (8, stage_line), (10, stage_mix), (10, stage_drain),
     )
 
     def step(i, _):
@@ -318,25 +466,15 @@
 
     lax.fori_loop(0, nz + stages[-1][0], step, 0)
 
-    def drain(j, _):
-        each(j, lambda dx: (dispatch(j, dx).wait_send(), give_back(j, dx).wait_send())[0])
-        own_up(j, t).wait_send()
-        own_down(j, t).wait_send()
-        on_up(j, down).wait_send()
-        on_down(j, up).wait_send()
-        for k, dy in enumerate((0, -1, 1, 2)):
-            across(j, k, tensor_peer(dy, c)).wait_send()
-        pair(j).wait_send()
-        for h in (0, 1):
-            hop(j, h).wait_send()
-            line(j, h).wait_send()
-        return 0
-
-    lax.fori_loop(0, nz, drain, 0)
+    result = total[...] + wide_total[y]
+    for dy in range(1, ny):
+        token_copy(dy, y).wait_send()
+        reduce(dy).wait()
+        result = result + red_in[dy - 1].astype(F32)
 
     keep = (1.0 - skipped_ref[...].astype(F32)) / jnp.sum(shares_ref[...].astype(F32), axis=0, keepdims=True)
     keep = jnp.sum(eye * keep, axis=1, keepdims=True)
-    out_ref[...] = (tokens_ref[...].astype(F32) + total[...] * keep).astype(BF16)
+    out_ref[...] = (tokens_ref[...].astype(F32) + result * keep).astype(BF16)
 
 
 def body(tokens, norm_gain, w_gate, w_up, w_down, routes, shares, skipped):
@@ -365,11 +503,14 @@
             pltpu.VMEM((local * ff, full), BF16),
             pltpu.VMEM((local * ff, full), BF16),
             pltpu.VMEM((nt, 8, tok), F32),
+            pltpu.VMEM((2 * ne, tok), F32),
+            pltpu.VMEM((2 * ne, tok), F32),
+            pltpu.VMEM((chunk, tok), F32),
             pltpu.VMEM((rows, tok), F32),
-            pltpu.VMEM((rows, tok), F32),
-            pltpu.VMEM((tok, feat), BF16),
+            pltpu.VMEM((ny, tok, feat), BF16),
             pltpu.VMEM((rows, feat), BF16),
-            pltpu.VMEM((nt, rows, feat), BF16),
+            pltpu.VMEM((ny, chunk, feat), BF16),
+            pltpu.VMEM((CORES, ny, rows, feat), BF16),
             pltpu.VMEM((2, chunk, local * ff), F32),
             pltpu.VMEM((CORES, ny, rows, feat), BF16),
             pltpu.VMEM((ny, rows, feat), BF16),
@@ -377,10 +518,18 @@
             pltpu.VMEM((2, rows, feat), BF16),
             pltpu.VMEM((rows, feat), BF16),
             pltpu.VMEM((rows, feat), BF16),
+            pltpu.VMEM((ny, chunk, feat), BF16),
             pltpu.VMEM((tok, feat), F32),
+            pltpu.VMEM((ny, tok, feat), F32),
+            pltpu.VMEM((ny - 1, tok, feat), BF16),
+            pltpu.VMEM((ny - 1, tok, feat), BF16),
             dma((3,)),
             dma((nt,)),
             dma((nt,)),
+            dma((ny,)),
+            dma((ny,)),
+            dma((ny - 1,)),
+            dma((ny - 1,)),
             dma((nz, nx)),
             dma((nz, nx)),
             dma((nz, 4)),

time: 148 us -> 142 us (0.959); the launches traced: 145 us -> 141 us
  Pallas kernels: 144 us -> 139 us
    pallas_call x1, Pallas kernels: 144 us -> 139 us  [body(): pl.pallas_call(functools.partial(kernel, nx, nz, ny, cap, full), out_shap...]
where the time goes in v4:
time: 142 us; the launch traced here: 141 us
  Pallas kernels  139 us (98%)
  local copies, waits for them, and re-layouts  1.57 us (1%)
    pallas_call x1, Pallas kernels, body(): pl.pallas_call(functools.partial(kernel, nx, nz, ny, cap, full), out_shap...  139 us

profile of v4, /device:TPU:8, one launch (start us, length us, event | category | flops | bytes accessed | tf_op | source)
XLA Modules:
  0.0 140.9 jit_solution(8033304905046864561)
XLA Ops:
  0.0 139.4 %shard_map.82 = bf16[128,512]{1,0:T(8,128)(2,1)} custom-call(bf16[128,512]{1,0:T(8,128)(2,1)} %tokens_ref.1, f32[32,128]{1,0:T(8,128)} %bitcast.10, s32[8,128]{1,0:T(8,128)} %bitcast.11, s32[8,128]{1,0:T(8,128)} %bitcast.12, s32[1,128]{1,0:T(1,128)} %bitcast.13, bf16[384,4096]{1,0:T(8,128)(2,1)} %bitcast.7, bf16[384,4096]{1,0:T(8,128)(2,1)} %bitcast.8, ...), custom_call_target="tpu_custom_call" | custom-call | tf_op jit(solution)/shard_map/pallas_call | solution.py:496
  139.4 1.6 %copy.10 = bf16[128,512]{1,0:T(8,128)(2,1)} copy(bf16[128,512]{1,0:T(8,128)(2,1)} %shard_map.82) | data formatting | bytes 262144

commit v5 on v4

--- a/solution.py
+++ b/solution.py
@@ -18,7 +18,7 @@
     nx, nz, ny, cap, full_feat,
     tokens_ref, gain_ref, routes_ref, shares_ref, skipped_ref, wg_hbm, wu_hbm, wd_hbm,
     out_ref,
-    wg, wu, wd, sums, slots, slot_share, pick, share, normed, outgoing, wide_out, rows_in, acc, part, pair_in, hop_in, line_in, done, back, wide_back, total, wide_total, red_out, red_in,
+    wg, wu, wd, sums, slots, slot_share, pick, share, normed, outgoing, wide_out, rows_in, acc, hidden, part, pair_in, hop_in, line_in, done, back, wide_back, total, wide_total, red_out, red_in,
     w_sem, sum_send, sum_recv, tok_send, tok_recv, red_send, red_recv, disp_send, disp_recv, ag_send, ag_recv, fw_send, fw_recv,
     pair_send, pair_recv, hop_send, hop_recv, line_send, line_recv, ret_send, ret_recv,
 ):
@@ -35,7 +35,7 @@
     y, c = t // CORES, t % CORES
     sib = y * CORES + (1 - c)
 
-    order = [nz - 1, 2, nz - 2, 4, 3, nz - 3, 1, 0] if nz == 8 else list(range(nz))
+    order = [nz - 1, 2, nz - 2, 4, 3, nz - 3, 0, 1] if nz == 8 else list(range(nz))
     local = order.index(0)
 
     def is_wide(j):
@@ -126,9 +126,6 @@
             device_id=(e, tensor_peer(dy, c)), device_id_type=MESH,
         )
 
-    for dy in range(1, ny):
-        token_copy(dy, y).start()
-
     def block(j, dx):
         return pl.ds(j * chunk + dx * blk, blk)
 
@@ -182,6 +179,11 @@
             for dx in range(nx):
                 dispatch(j, dx).start()
 
+        @pl.when(j == 1)
+        def _():
+            for dy in range(1, ny):
+                token_copy(dy, y).start()
+
         @pl.when(j == local)
         def _():
             for dy in range(1, ny):
@@ -323,13 +325,16 @@
         first_row = lax.broadcasted_iota(jnp.int32, (chunk, two), 0) % blk < cap
         first_col = lax.broadcasted_iota(jnp.int32, (chunk, two), 1) < two // 2
         gate = acc[0]
-        hidden = gate * jax.nn.sigmoid(gate) * acc[1]
-        hidden = jnp.where(first_row == first_col, hidden, 0.0).astype(BF16)
+        mixed = gate * jax.nn.sigmoid(gate) * acc[1]
+        hidden[...] = jnp.where(first_row == first_col, mixed, 0.0).astype(BF16)
+
+    def stage_narrow(j):
+        rows = whole(j)
 
         def narrow(s, _):
             cols = pl.ds(pl.multiple_of(s * feat, feat), feat)
             part[s % CORES, s // CORES, rows, :] = jnp.dot(
-                hidden, wd[:, cols], preferred_element_type=F32
+                hidden[...], wd[:, cols], preferred_element_type=F32
             ).astype(BF16)
             return 0
 
@@ -452,8 +457,17 @@
     total[...] = jnp.zeros_like(total)
     wide_total[...] = jnp.zeros_like(wide_total)
     stages = (
-        (0, stage_send), (2, stage_gather), (3, stage_forward), (4, stage_far), (5, stage_expert),
-        (6, stage_pair), (7, stage_hop), (8, stage_line), (10, stage_mix), (10, stage_drain),
+        (0, stage_send),
+        (2, stage_gather),
+        (3, stage_forward),
+        (4, stage_far),
+        (5, stage_expert),
+        (7, stage_hop),
+        (8, stage_line),
+        (5, stage_narrow),
+        (6, stage_pair),
+        (10, stage_mix),
+        (10, stage_drain),
     )
 
     def step(i, _):
@@ -512,6 +526,7 @@
             pltpu.VMEM((ny, chunk, feat), BF16),
             pltpu.VMEM((CORES, ny, rows, feat), BF16),
             pltpu.VMEM((2, chunk, local * ff), F32),
+            pltpu.VMEM((chunk, local * ff), BF16),
             pltpu.VMEM((CORES, ny, rows, feat), BF16),
             pltpu.VMEM((ny, rows, feat), BF16),
             pltpu.VMEM((2, rows // 2, feat), BF16),

time: 142 us -> 140 us (0.986)
  Pallas kernels: 139 us -> 137 us
    pallas_call x1, Pallas kernels: 139 us -> 137 us  [body(): pl.pallas_call(functools.partial(kernel, nx, nz, ny, cap, full), out_shap...]
where the time goes in v5:
time: 140 us; the launch traced here: 139 us
  Pallas kernels  137 us (98%)
  local copies, waits for them, and re-layouts  1.57 us (1%)
    pallas_call x1, Pallas kernels, body(): pl.pallas_call(functools.partial(kernel, nx, nz, ny, cap, full), out_shap...  137 us

profile of v5, /device:TPU:8, one launch (start us, length us, event | category | flops | bytes accessed | tf_op | source)
XLA Modules:
  0.0 138.8 jit_solution(1806140285034965282)
XLA Ops:
  0.0 137.2 %shard_map.82 = bf16[128,512]{1,0:T(8,128)(2,1)} custom-call(bf16[128,512]{1,0:T(8,128)(2,1)} %tokens_ref.1, f32[32,128]{1,0:T(8,128)} %bitcast.10, s32[8,128]{1,0:T(8,128)} %bitcast.11, s32[8,128]{1,0:T(8,128)} %bitcast.12, s32[1,128]{1,0:T(1,128)} %bitcast.13, bf16[384,4096]{1,0:T(8,128)(2,1)} %bitcast.7, bf16[384,4096]{1,0:T(8,128)(2,1)} %bitcast.8, ...), custom_call_target="tpu_custom_call" | custom-call | tf_op jit(solution)/shard_map/pallas_call | solution.py:510
  137.2 1.6 %copy.10 = bf16[128,512]{1,0:T(8,128)(2,1)} copy(bf16[128,512]{1,0:T(8,128)(2,1)} %shard_map.82) | data formatting | bytes 262144
